TPU v7x, 32 devices: a whole 2x2x4 slice. The times are simulated.
32 devices in a mesh: frame: 4 (over x, core), band: 8 (over z, y).
Axes of the slice: x: 2, y: 2, z: 4, core: 2. Of those that a mesh axis runs over, the one named last changes fastest.
Arguments:
- noisy_snapshot_stack: bfloat16 [4, 8, 180, 512], P('frame', 'band'), may hold values from -6 to 6
- gaussian_perturbation: bfloat16 [4, 8, 180, 512], P('frame', 'band'), may hold values from -6 to 6
- snapshot_noise_indices: int32 [4], P('frame'), may hold values from 0 to 3, each once
- partition_longitude_starts: int32 [4], P('frame'), may hold values from 0 to 59
- latitude_patch_tally: int32 [8], replicated, may hold values from 90 to 180
- normalizer_scaling: float32 [512], replicated, may hold values from 0.1 to 1.9
- head_score_scales: float32 [2, 8], replicated, may hold values from 0.5 to 100
- local_projection_matrices: bfloat16 [512, 1536], P(None, 'band'), may hold values from -0.25 to 0.25
- time_projection_matrices: bfloat16 [512, 1536], P(None, 'band'), may hold values from -0.25 to 0.25
- final_projection_matrices: bfloat16 [1024, 512], P(None, 'band'), may hold values from -0.1875 to 0.1875
Outputs:
- next_state: bfloat16 [4, 8, 180, 512], P('frame', 'band')
Inputs may be any that keep to these rules, and one draw needn't show every extreme that they name: `snapshot_noise_indices`: each level index 0 to 3 belongs to exactly one frame.
All inputs are finite; a program needn't handle non-finite values.
Results may differ from a plain program's by a relative error of at most 0.0071.
Values may be sent and summed in bfloat16 or wider, within the bound.
No kernel may reach another device: no remote copies, remote signals or barrier semaphores. Data moves between devices by JAX's collectives and lax.ppermute only.
A program may use at most 64 MiB of HBM per device.

v0:
```python
import math
import jax
import jax.numpy as jnp
from jax import lax
from jax.sharding import PartitionSpec as P

HEADS = 8
HEAD_DIM = 64
WINDOW = 60
PRIOR_SNAPSHOTS = 3
epsilon = 1e-06
sigma_low = 0.1
sigma_high = 2.0
keep_share = 0.8
fresh_share = 0.6


def extended(cells, sides, width):
    for axis, dim in sides:
        count = lax.axis_size(axis)
        ends = count - 1
        head = lax.slice_in_dim(cells, 0, width, axis=dim)
        tail = lax.slice_in_dim(cells, cells.shape[dim] - width, cells.shape[dim], axis=dim)
        cells = jnp.concatenate(
            [
                lax.ppermute(tail, axis, [(i, (i + 1) % count) for i in range(ends)]),
                cells,
                lax.ppermute(head, axis, [((i + 1) % count, i) for i in range(ends)]),
            ],
            axis=dim,
        )
    return cells


def shifted(block, axis, distance):
    devices = range(lax.axis_size(axis))
    route = [(i - distance, i) for i in devices if i - distance in devices]
    return lax.ppermute(block, axis, route)


def sigma_of(level, total_levels):
    return sigma_low * jnp.power(
        sigma_high / sigma_low, (level.astype(jnp.float32) + 1.0) / total_levels
    )


def unit_heads(content_vectors):
    shaped = content_vectors.reshape(content_vectors.shape[:-1] + (HEADS, HEAD_DIM))
    scale = lax.rsqrt(jnp.mean(shaped * shaped, axis=-1, keepdims=True) + epsilon)
    return (shaped * scale).reshape(content_vectors.shape)


def pick(table, index):
    return jnp.sum(jnp.where(jnp.arange(table.shape[0]) == index, table, 0))


def with_past(local, frame_dim, shifter):
    frames = local.shape[frame_dim]
    hops = -(-PRIOR_SNAPSHOTS // frames)
    pieces = [shifter(local, hop) for hop in range(hops, 0, -1)]
    joined = jnp.concatenate(pieces + [local], axis=frame_dim)
    return joined


def local_patch_mixer(
    asking_vectors,
    fringe_lookup_vectors,
    fringe_content_vectors,
    fringe_present_flags,
    snapshot_longitude_shift,
    temper,
):
    rows, lon, token_extent = asking_vectors.shape
    wins = lon // WINDOW
    asking_vectors = jnp.roll(asking_vectors, -snapshot_longitude_shift, axis=1).reshape(
        rows, wins, WINDOW, HEADS, HEAD_DIM
    )
    fringe_lookup_vectors = jnp.roll(
        fringe_lookup_vectors, -snapshot_longitude_shift, axis=1
    ).reshape(rows + 2, wins, WINDOW, HEADS, HEAD_DIM)
    fringe_content_vectors = jnp.roll(
        fringe_content_vectors, -snapshot_longitude_shift, axis=1
    ).reshape(rows + 2, wins, WINDOW, HEADS, HEAD_DIM)
    fringe_present_flags = jnp.roll(
        fringe_present_flags, -snapshot_longitude_shift, axis=1
    ).reshape(rows + 2, wins, WINDOW)
    lookup_vectors = jnp.concatenate(
        [fringe_lookup_vectors[:-2], fringe_lookup_vectors[1:-1], fringe_lookup_vectors[2:]], axis=2
    )
    content_vectors = jnp.concatenate(
        [fringe_content_vectors[:-2], fringe_content_vectors[1:-1], fringe_content_vectors[2:]],
        axis=2,
    )
    permitted_mask = jnp.concatenate(
        [fringe_present_flags[:-2], fringe_present_flags[1:-1], fringe_present_flags[2:]], axis=2
    )
    inner = jnp.arange(WINDOW)
    middle = jnp.arange(3 * WINDOW)
    itself = middle[None, :] == inner[:, None] + WINDOW
    permitted_mask = permitted_mask[:, :, None, None, :] | itself[None, None, None]
    scores = jnp.einsum(
        "rwqhd,rwkhd->rwhqk", asking_vectors, lookup_vectors, preferred_element_type=jnp.float32
    )
    scores = scores * (temper / math.sqrt(HEAD_DIM))[None, None, :, None, None]
    top = jnp.max(jnp.where(permitted_mask, scores, -jnp.inf), axis=-1, keepdims=True)
    weights = jnp.where(permitted_mask, jnp.exp(scores - top), 0.0)
    probs = (weights / jnp.sum(weights, axis=-1, keepdims=True)).astype(jnp.bfloat16)
    combined_result_field = jnp.einsum(
        "rwhqk,rwkhd->rwqhd", probs, content_vectors, preferred_element_type=jnp.float32
    )
    combined_result_field = combined_result_field.reshape(rows, lon, token_extent)
    return jnp.roll(combined_result_field, snapshot_longitude_shift, axis=1).astype(jnp.bfloat16)


def across_time_mixer(asking_vectors, lookup_vectors, content_vectors, permitted_mask, temper):
    count, token_extent = asking_vectors.shape
    span = lookup_vectors.shape[0]
    query_heads = asking_vectors.reshape(count, HEADS, HEAD_DIM)
    key_heads = lookup_vectors.reshape(span, count, HEADS, HEAD_DIM)
    value_heads = content_vectors.reshape(span, count, HEADS, HEAD_DIM)
    scores = jnp.einsum("thd,jthd->jht", query_heads, key_heads, preferred_element_type=jnp.float32)
    scores = scores * (temper / math.sqrt(HEAD_DIM))[None, :, None]
    top = jnp.max(jnp.where(permitted_mask, scores, -jnp.inf), axis=0, keepdims=True)
    weights = jnp.where(permitted_mask, jnp.exp(scores - top), 0.0)
    probs = (weights / jnp.sum(weights, axis=0, keepdims=True)).astype(jnp.bfloat16)
    combined_result_field = jnp.einsum(
        "jht,jthd->thd", probs, value_heads, preferred_element_type=jnp.float32
    )
    return combined_result_field.reshape(count, token_extent).astype(jnp.bfloat16)


def body(
    noisy_snapshot_stack,
    gaussian_perturbation,
    snapshot_noise_indices,
    partition_longitude_starts,
    latitude_patch_tally,
    normalizer_scaling,
    head_score_scales,
    local_projection_matrices,
    time_projection_matrices,
    final_projection_matrices,
):
    frames, rows, lon, token_extent = noisy_snapshot_stack.shape
    token_grid = frames * rows * lon
    band = lax.axis_index("band")
    frame_base = lax.axis_index("frame") * frames
    total_levels = lax.axis_size("frame") * frames
    state_f = noisy_snapshot_stack.astype(jnp.float32)
    normed = (
        state_f
        * lax.rsqrt(jnp.mean(state_f * state_f, axis=-1, keepdims=True) + epsilon)
        * normalizer_scaling
    ).astype(jnp.bfloat16)
    margin = 0
    space_rows = normed.reshape(-1, token_extent)
    space_proj = jnp.dot(
        space_rows,
        lax.all_gather(local_projection_matrices, "band", axis=1, tiled=True),
        preferred_element_type=jnp.float32,
    )
    space_proj = space_proj.reshape(frames, rows + 2 * margin, lon, 3 * token_extent)
    window_queries = unit_heads(space_proj[:, margin : margin + rows, :, :token_extent]).astype(
        jnp.bfloat16
    )
    space_key = unit_heads(space_proj[..., token_extent : 2 * token_extent]).astype(jnp.bfloat16)
    space_value = space_proj[..., 2 * token_extent :].astype(jnp.bfloat16)
    stacked = extended(jnp.stack([space_key, space_value]), (("band", 2),), 1)
    fringe_lookup_vectors = stacked[0]
    fringe_content_vectors = stacked[1]
    plane = rows * lon
    time_rows = normed.reshape(-1, token_extent)
    time_proj = jnp.dot(
        time_rows,
        lax.all_gather(time_projection_matrices, "band", axis=1, tiled=True),
        preferred_element_type=jnp.float32,
    )
    span = PRIOR_SNAPSHOTS + 1
    time_proj = time_proj.reshape(normed.shape[0], rows, lon, 3 * token_extent)
    temporal_queries = unit_heads(time_proj[-frames:, :, :, :token_extent]).astype(jnp.bfloat16)
    time_key = unit_heads(time_proj[..., token_extent : 2 * token_extent]).astype(jnp.bfloat16)
    time_value = time_proj[..., 2 * token_extent :].astype(jnp.bfloat16)

    def shift_values(block, hop):
        return shifted(block, "frame", hop)

    joined = with_past(jnp.stack([time_key, time_value]), 1, shift_values)
    keys_all = joined[0]
    values_all = joined[1]
    key_columns = jnp.stack([keys_all[j : j + frames] for j in range(span)]).reshape(
        span, token_grid, token_extent
    )
    value_columns = jnp.stack([values_all[j : j + frames] for j in range(span)]).reshape(
        span, token_grid, token_extent
    )
    frame_of = jnp.arange(token_grid) // plane
    position = frame_base + frame_of[None, :] - PRIOR_SNAPSHOTS + jnp.arange(span)[:, None]
    permitted_mask = (position >= 0)[:, None, :]
    time_mix = across_time_mixer(
        temporal_queries.reshape(token_grid, token_extent),
        key_columns,
        value_columns,
        permitted_mask,
        head_score_scales[1],
    )
    inner = jnp.arange(rows)[:, None] * lon + jnp.arange(lon)[None, :]
    own_valid = inner < pick(latitude_patch_tally, band)
    above = inner < pick(latitude_patch_tally, band - 1)
    below = inner < pick(latitude_patch_tally, band + 1)
    fringe_present_flags = jnp.concatenate([above, own_valid, below], axis=0)
    space_parts = [
        local_patch_mixer(
            window_queries[0],
            fringe_lookup_vectors[0],
            fringe_content_vectors[0],
            fringe_present_flags,
            partition_longitude_starts[0],
            head_score_scales[0],
        )
    ]
    space_mix = jnp.stack(space_parts).reshape(token_grid, token_extent)
    mixed = jnp.concatenate([space_mix, time_mix], axis=1)
    update = jnp.dot(
        mixed,
        lax.all_gather(final_projection_matrices, "band", axis=1, tiled=True),
        preferred_element_type=jnp.float32,
    ).reshape(frames, rows, lon, token_extent)
    sigma = sigma_of(snapshot_noise_indices, total_levels)[:, None, None, None]
    sigma_next = sigma_of(snapshot_noise_indices - 1, total_levels)[:, None, None, None]
    denoised = state_f / (1.0 + sigma * sigma) + sigma * lax.rsqrt(1.0 + sigma * sigma) * update
    noise_f = gaussian_perturbation.astype(jnp.float32)
    stepped = denoised + sigma_next * (
        keep_share * (state_f - denoised) / sigma + fresh_share * noise_f
    )
    finished = (snapshot_noise_indices == 0)[:, None, None, None]
    return jnp.where(finished, sigma_high * noise_f, stepped).astype(jnp.bfloat16)


def solution(mesh):
    return jax.shard_map(
        body,
        mesh=mesh,
        in_specs=(
            P("frame", "band", None, None),
            P("frame", "band", None, None),
            P("frame"),
            P("frame"),
            P(),
            P(),
            P(),
            P(None, "band"),
            P(None, "band"),
            P(None, "band"),
        ),
        out_specs=P("frame", "band", None, None),
        check_vma=False,
    )
```

profile of v0, /device:TPU:0, one launch (start us, length us, event | category | flops | bytes accessed | tf_op | source)
XLA Modules:
  0.0 159.1 jit_solution(10543922075528884963)
XLA Ops:
  6.5 0.7 all-gather.4.cloned.1.call-update
  7.3 0.7 all-gather.6.cloned.1.call-update
  8.1 0.7 all-gather.8.cloned.1.call-update
  9.4 1.0 fusion.24
  10.5 0.8 multiply_bitcast_fusion.1
  11.3 1.4 fusion.55
  12.6 0.7 iota_compare_fusion.4
  13.3 1.3 iota_compare_fusion.2
  16.0 40.5 %all-gather.4.cloned.1.call-done = bf16[512,1536]{0,1:T(8,128)(2,1)} async-done(((bf16[512,192]{0,1:T(8,128)(2,1)}), bf16[512,1536]{0,1:T(8,128)(2,1)}) %all-gather.4.cloned.1.call-update) | async-done | bytes 1572880 | tf_op jit(solution)/shard_map/all_gather | solution.py:159
  56.5 2.2 %convolution_bitcast_fusion.1 = f32[1,1,180,1536]{3,2,1,0:T(8,128)S(1)} fusion(bf16[512,1536]{0,1:T(8,128)(2,1)} %all-gather.4.cloned.1.call-done, bf16[1,1,180,512]{3,2,1,0:T(8,128)(2,1)} %param.12, f32[512]{0:T(512)} %param.17, f32[180]{0:T(256)S(1)} %add_rsqrt_fusion.4), kind=kOutput, calls=%fused_computation.2 | convolution fusion | flops 283484160 | bytes 2865872 | tf_op jit(solution)/shard_map/dot_general | solution.py:157
  58.8 0.2 copy.43
  59.1 0.2 copy.44
  59.3 0.2 copy.48
  59.6 0.2 copy.49
  59.8 0.8 fusion.36
  60.6 0.8 pad_maximum_fusion.1
  61.4 3.2 %collective-permute-start = (bf16[2,1,1,180,512]{4,3,2,1,0:T(8,128)(2,1)}, bf16[2,1,1,180,512]{4,3,2,1,0:T(8,128)(2,1)}, u32[]{:S(2)}, u32[]{:S(2)}) collective-permute-start(bf16[2,1,1,180,512]{4,3,2,1,0:T(8,128)(2,1)} %pad_maximum_fusion.1), channel_id=1, source_target_pairs={{0,1},{1,2},{2,3},{3,4},{4,5},{5,6},{6,7},{8,9},{9,10},{10,11},{11... | collective-permute-start | bytes 1105928 | tf_op jit(solution)/shard_map/ppermute | solution.py:26
  64.6 1.3 collective-permute-start.1
  65.9 43.0 %all-gather.6.cloned.1.call-done = bf16[512,1536]{0,1:T(8,128)(2,1)} async-done(((bf16[512,192]{0,1:T(8,128)(2,1)}), bf16[512,1536]{0,1:T(8,128)(2,1)}) %all-gather.6.cloned.1.call-update) | async-done | bytes 1572880 | tf_op jit(solution)/shard_map/all_gather | solution.py:175
  108.8 2.1 %convolution_bitcast_fusion = f32[1,1,180,1536]{3,2,1,0:T(8,128)S(1)} fusion(bf16[512,1536]{0,1:T(8,128)(2,1)} %all-gather.6.cloned.1.call-done, bf16[1,1,180,512]{3,2,1,0:T(8,128)(2,1)S(1)} %copy-done, f32[512]{0:T(512)S(1)} %copy-done.4, f32[180]{0:T(256)S(1)} %add_rsqrt_fusion.4), kind=kOutput, calls=%fused_computation.1 | convolution fusion | flops 283484160 | bytes 2865872 | tf_op jit(solution)/shard_map/dot_general | solution.py:173
  111.0 0.2 copy.55
  111.3 0.2 copy.56
  111.5 0.2 copy.61
  111.8 0.2 copy.62
  112.0 0.2 multiply_convert_fusion
  112.2 0.8 pad_maximum_fusion.2
  113.0 2.9 %collective-permute-start.2 = (bf16[2,1,1,180,512]{4,3,2,1,0:T(8,128)(2,1)}, bf16[2,1,1,180,512]{4,3,2,1,0:T(8,128)(2,1)}, u32[]{:S(2)}, u32[]{:S(2)}) collective-permute-start(bf16[2,1,1,180,512]{4,3,2,1,0:T(8,128)(2,1)} %pad_maximum_fusion.2), channel_id=1, source_target_pairs={{0,24},{1,25},{2,26},{3,27},{4,28},{5,29},{6,30},{7,31}} | collective-permute-start | bytes 1105928 | tf_op jit(solution)/shard_map/ppermute | solution.py:38
  115.9 2.6 %collective-permute-start.3 = (bf16[2,1,1,180,512]{4,3,2,1,0:T(8,128)(2,1)}, bf16[2,1,1,180,512]{4,3,2,1,0:T(8,128)(2,1)}, u32[]{:S(2)}, u32[]{:S(2)}) collective-permute-start(bf16[2,1,1,180,512]{4,3,2,1,0:T(8,128)(2,1)} %pad_maximum_fusion.2), channel_id=1, source_target_pairs={{0,16},{8,24},{1,17},{9,25},{2,18},{10,26},{3,19},{11,27},{4,20},{... | collective-permute-start | bytes 1105928 | tf_op jit(solution)/shard_map/ppermute | solution.py:38
  118.5 2.0 %collective-permute-start.4 = (bf16[2,1,1,180,512]{4,3,2,1,0:T(8,128)(2,1)}, bf16[2,1,1,180,512]{4,3,2,1,0:T(8,128)(2,1)}, u32[]{:S(2)}, u32[]{:S(2)}) collective-permute-start(bf16[2,1,1,180,512]{4,3,2,1,0:T(8,128)(2,1)} %pad_maximum_fusion.2), channel_id=1, source_target_pairs={{0,8},{8,16},{16,24},{1,9},{9,17},{17,25},{2,10},{10,18},{18,26},{... | collective-permute-start | bytes 1105928 | tf_op jit(solution)/shard_map/ppermute | solution.py:38
  120.7 0.4 fusion.34
  121.1 0.2 reshape.379
  121.3 0.1 copy.82
  121.5 0.8 copy.67
  122.3 1.2 pad_maximum_fusion
  123.7 1.2 fusion.16
  124.9 0.2 slice.150
  125.1 0.3 copy.50
  125.4 0.2 slice.152
  125.7 0.3 copy.51
  126.0 0.2 slice.154
  126.2 0.3 copy.52
  126.6 0.8 convolution_multiply_fusion
  127.3 1.7 %fusion.67 = (f32[3,8,60]{2,1,0:T(8,128)S(1)}, f32[3,8,60,180]{3,2,1,0:T(8,128)}) fusion(f32[3,8,60,180]{3,2,1,0:T(8,128)S(1)} %convolution_multiply_fusion, pred[3,60,180]{2,1,0:T(8,128)(4,1)S(1)} %broadcast_or_fusion), kind=kOutput, calls=%fused_computation.140 | output fusion | flops 1036979 | bytes 2111760 | tf_op jit(solution)/shard_map/sub | solution.py:106
  129.0 0.2 slice.136
  129.3 1.1 copy.45
  130.3 0.2 slice.138
  130.5 1.1 copy.46
  131.6 0.2 slice.140
  131.8 0.3 copy.47
  132.1 2.7 %convolution_bitcast_fusion.2 = bf16[1,3,60,8,64]{2,4,3,1,0:T(8,128)(2,1)} fusion(bf16[1,3,60,8,64]{2,4,3,1,0:T(8,128)(2,1)S(1)} %copy.47, bf16[1,3,60,8,64]{2,4,3,1,0:T(8,128)(2,1)} %copy.46, bf16[1,3,60,8,64]{2,4,3,1,0:T(8,128)(2,1)} %copy.45, f32[3,8,60,180]{3,2,1,0:T(8,128)S(1)} %copy-done.1, f32[3,8,60]{2,1,0:T(8,128)S(1)} %get-tuple-element.36), kind=kOutput, calls=%fused_computation.10 | convolution fusion | flops 35354880 | bytes 1779840 | tf_op jit(solution)/shard_map/rwhqk,rwkhd->rwqhd/dot_general | solution.py:108
  134.8 1.3 copy.54
  136.1 0.2 reshape.381
  136.3 1.0 fusion.64
  137.5 1.0 fusion.65
  138.6 0.1 copy.58
  138.7 1.1 fusion.66
  139.8 0.1 copy.59
  139.9 0.1 copy.64
  140.1 0.1 copy.65
  140.4 0.3 multiply_reduce_fusion.1
  141.0 0.3 multiply_reduce_fusion
  141.4 0.4 fusion.38
  141.8 8.2 %all-gather.8.cloned.1.call-done = bf16[1024,512]{0,1:T(8,128)(2,1)} async-done(((bf16[1024,64]{0,1:T(8,128)(2,1)}), bf16[1024,512]{0,1:T(8,128)(2,1)}) %all-gather.8.cloned.1.call-update) | async-done | bytes 1048592 | tf_op jit(solution)/shard_map/all_gather | solution.py:225
  150.0 2.5 %fusion.20 = bf16[1,1,180,512]{3,2,1,0:T(8,128)(2,1)} fusion(bf16[1,1,180,512]{3,2,1,0:T(8,128)(2,1)S(1)} %copy-done.5, bf16[1,1,180,512]{3,2,1,0:T(8,128)(2,1)S(1)} %copy-done, bf16[1024,512]{0,1:T(8,128)(2,1)} %all-gather.8.cloned.1.call-done, bf16[180,512]{1,0:T(8,128)(2,1)S(1)} %copy.68, bf16[180,512]{1,0:T(8,128)(2,1)S(1)} %fusion.38, f32[]{:T(128)} %bitcast.51, ...), kind=kOutput, calls=%fused_computation.47 | convolution fusion | flops 190863360 | bytes 1970193 | tf_op jit(solution)/shard_map/dot_general | solution.py:223
  (60 shorter events, 2.3 us)
Async XLA Ops:
  6.5 49.9 %all-gather.4.cloned.1.call-start = ((), (), s32[]{:S(2)}) async-start(), calls=%async_computation | async-start | bytes 1769472 | tf_op jit(solution)/shard_map/all_gather | solution.py:159
  7.3 101.6 %all-gather.6.cloned.1.call-start = ((), (), s32[]{:S(2)}) async-start(), calls=%async_computation.1 | async-start | bytes 1769472 | tf_op jit(solution)/shard_map/all_gather | solution.py:175
  8.0 142.0 %all-gather.8.cloned.1.call-start = ((), (), s32[]{:S(2)}) async-start(), calls=%async_computation.2 | async-start | bytes 1179648 | tf_op jit(solution)/shard_map/all_gather | solution.py:225
  59.6 49.2 %copy-start = (bf16[1,1,180,512]{3,2,1,0:T(8,128)(2,1)S(1)}, bf16[1,1,180,512]{3,2,1,0:T(8,128)(2,1)}, u32[]{:S(2)}) copy-start(bf16[1,1,180,512]{3,2,1,0:T(8,128)(2,1)} %param.12) | copy-start | bytes 552964
  59.6 49.2 %copy-start.4 = (f32[512]{0:T(512)S(1)}, f32[512]{0:T(512)}, u32[]{:S(2)}) copy-start(f32[512]{0:T(512)} %param.17) | copy-start | bytes 6148
  61.4 61.0 %collective-permute-start = (bf16[2,1,1,180,512]{4,3,2,1,0:T(8,128)(2,1)}, bf16[2,1,1,180,512]{4,3,2,1,0:T(8,128)(2,1)}, u32[]{:S(2)}, u32[]{:S(2)}) collective-permute-start(bf16[2,1,1,180,512]{4,3,2,1,0:T(8,128)(2,1)} %pad_maximum_fusion.1), channel_id=1, source_target_pairs={{0,1},{1,2},{2,3},{3,4},{4,5},{5,6},{6,7},{8,9},{9,10},{10,11},{11... | collective-permute-start | bytes 1105928 | tf_op jit(solution)/shard_map/ppermute | solution.py:26
  64.6 57.8 %collective-permute-start.1 = (bf16[2,1,1,180,512]{4,3,2,1,0:T(8,128)(2,1)}, bf16[2,1,1,180,512]{4,3,2,1,0:T(8,128)(2,1)}, u32[]{:S(2)}, u32[]{:S(2)}) collective-permute-start(bf16[2,1,1,180,512]{4,3,2,1,0:T(8,128)(2,1)} %pad_maximum_fusion.1), channel_id=1, source_target_pairs={{1,0},{2,1},{3,2},{4,3},{5,4},{6,5},{7,6},{9,8},{10,9},{11,10},{12... | collective-permute-start | bytes 1105928 | tf_op jit(solution)/shard_map/ppermute | solution.py:28
  112.0 8.7 %copy-start.3 = (bf16[1,180,512]{2,1,0:T(8,128)(2,1)S(1)}, bf16[1,180,512]{2,1,0:T(8,128)(2,1)}, u32[]{:S(2)}) copy-start(bf16[1,180,512]{2,1,0:T(8,128)(2,1)} %get-tuple-element.12) | copy-start | bytes 552964
  113.0 23.3 %collective-permute-start.2 = (bf16[2,1,1,180,512]{4,3,2,1,0:T(8,128)(2,1)}, bf16[2,1,1,180,512]{4,3,2,1,0:T(8,128)(2,1)}, u32[]{:S(2)}, u32[]{:S(2)}) collective-permute-start(bf16[2,1,1,180,512]{4,3,2,1,0:T(8,128)(2,1)} %pad_maximum_fusion.2), channel_id=1, source_target_pairs={{0,24},{1,25},{2,26},{3,27},{4,28},{5,29},{6,30},{7,31}} | collective-permute-start | bytes 1105928 | tf_op jit(solution)/shard_map/ppermute | solution.py:38
  115.9 21.6 %collective-permute-start.3 = (bf16[2,1,1,180,512]{4,3,2,1,0:T(8,128)(2,1)}, bf16[2,1,1,180,512]{4,3,2,1,0:T(8,128)(2,1)}, u32[]{:S(2)}, u32[]{:S(2)}) collective-permute-start(bf16[2,1,1,180,512]{4,3,2,1,0:T(8,128)(2,1)} %pad_maximum_fusion.2), channel_id=1, source_target_pairs={{0,16},{8,24},{1,17},{9,25},{2,18},{10,26},{3,19},{11,27},{4,20},{... | collective-permute-start | bytes 1105928 | tf_op jit(solution)/shard_map/ppermute | solution.py:38
  118.5 20.2 %collective-permute-start.4 = (bf16[2,1,1,180,512]{4,3,2,1,0:T(8,128)(2,1)}, bf16[2,1,1,180,512]{4,3,2,1,0:T(8,128)(2,1)}, u32[]{:S(2)}, u32[]{:S(2)}) collective-permute-start(bf16[2,1,1,180,512]{4,3,2,1,0:T(8,128)(2,1)} %pad_maximum_fusion.2), channel_id=1, source_target_pairs={{0,8},{8,16},{16,24},{1,9},{9,17},{17,25},{2,10},{10,18},{18,26},{... | collective-permute-start | bytes 1105928 | tf_op jit(solution)/shard_map/ppermute | solution.py:38
  129.2 2.9 %copy-start.1 = (f32[3,8,60,180]{3,2,1,0:T(8,128)S(1)}, f32[3,8,60,180]{3,2,1,0:T(8,128)}, u32[]{:S(2)}) copy-start(f32[3,8,60,180]{3,2,1,0:T(8,128)} %get-tuple-element.37) | copy-start | bytes 3110404
  139.9 1.0 copy-start.2
  140.7 9.3 %copy-start.5 = (bf16[1,1,180,512]{3,2,1,0:T(8,128)(2,1)S(1)}, bf16[1,1,180,512]{3,2,1,0:T(8,128)(2,1)}, u32[]{:S(2)}) copy-start(bf16[1,1,180,512]{3,2,1,0:T(8,128)(2,1)} %param.13) | copy-start | bytes 552964
Sparse Core Ops, SparseCore 0:
  9.5 46.8 all-gather.3
  58.6 50.1 all-gather.5
  111.0 39.0 all-gather.7
where the time goes:
time: 160 us; the launch traced here: 159 us
  waiting for transfers between devices  93.8 us (59%)
  between operations  15.2 us (10%)
  other arithmetic  14 us (9%)
  local copies, waits for them, and re-layouts  13.8 us (9%)
  starting transfers between devices  12.1 us (8%)
  matrix products  10.2 us (6%)
    all_gather x1, waiting for transfers between devices, body(): lax.all_gather(time_projection_matrices, 'band', axis=1, tiled=True)  43 us
    all_gather x1, waiting for transfers between devices, body(): lax.all_gather(local_projection_matrices, 'band', axis=1, tiled=True)  40.5 us
    all_gather x1, waiting for transfers between devices, body(): lax.all_gather(final_projection_matrices, 'band', axis=1, tiled=True)  8.25 us
    ppermute x3, starting transfers between devices, shifted(): return lax.ppermute(block, axis, route)  7.54 us
    slice x6, local copies, waits for them, and re-layouts, body(): keys_all[j:j + frames]  3.53 us
  transfers between devices with their start and end apart: 8, of which 3 were waited for; matrix products, arithmetic and copies ran while one was open for 22% of the time, Pallas kernels for 0%

commit v1 on v0

--- a/solution.py
+++ b/solution.py
@@ -1,8 +1,10 @@
+import functools
 import math
 import jax
 import jax.numpy as jnp
 from jax import lax
 from jax.sharding import PartitionSpec as P
+from jax.lax import axis_index, axis_size, ppermute
 
 HEADS = 8
 HEAD_DIM = 64
@@ -13,6 +15,30 @@
 sigma_high = 2.0
 keep_share = 0.8
 fresh_share = 0.6
+
+
+def _attach_case(x_part, on_dim):
+    x_part = jnp.moveaxis(x_part, 0, on_dim)
+    e_next = x_part.shape
+    earlier = x_part.reshape(
+        *e_next[:on_dim], e_next[on_dim] * e_next[on_dim + 1], *e_next[on_dim + 2 :]
+    )
+    return earlier
+
+
+def _convert_stocks(shard_in, mesh_dim, where_dim):
+    ndev = axis_size(mesh_dim)
+    row_list = [(w, (w + 1) % ndev) for w in range(ndev)]
+    column = [shard_in]
+    while len(column) < ndev:
+        column.append(ppermute(column[-1], axis_name=mesh_dim, perm=row_list))
+    y_new = axis_index(mesh_dim)
+    column = jnp.stack(column)[(y_new - jnp.arange(ndev)) % ndev]
+    item_now = _attach_case(column, where_dim)
+    return item_now
+
+
+rest_the_row = functools.partial(_convert_stocks, mesh_dim="band", where_dim=1)
 
 
 def extended(cells, sides, width):
@@ -155,9 +181,7 @@
     margin = 0
     space_rows = normed.reshape(-1, token_extent)
     space_proj = jnp.dot(
-        space_rows,
-        lax.all_gather(local_projection_matrices, "band", axis=1, tiled=True),
-        preferred_element_type=jnp.float32,
+        space_rows, rest_the_row(local_projection_matrices), preferred_element_type=jnp.float32
     )
     space_proj = space_proj.reshape(frames, rows + 2 * margin, lon, 3 * token_extent)
     window_queries = unit_heads(space_proj[:, margin : margin + rows, :, :token_extent]).astype(

time: 160 us -> 147 us (0.919)
  the two profiles are of different devices: /device:TPU:0 before, /device:TPU:18 now
where the time goes in v1:
time: 147 us
  waiting for transfers between devices  75.5 us (51%)
  local copies, waits for them, and re-layouts  19.9 us (14%)
  between operations  15.6 us (11%)
  starting transfers between devices  15.4 us (10%)
  other arithmetic  12.7 us (9%)
  matrix products  7.59 us (5%)
    ppermute x7, waiting for transfers between devices, _convert_stocks(): column.append(ppermute(column[-1], axis_name=mesh_dim, perm=row_list))  51.9 us
    ppermute x1, waiting for transfers between devices, extended(): lax.ppermute(tail, axis, [(i, (i + 1) % count) for i in range(ends)])  9.7 us
    ppermute x3, waiting for transfers between devices, shifted(): return lax.ppermute(block, axis, route)  7.36 us
    ppermute x1, waiting for transfers between devices, extended(): lax.ppermute(head, axis, [((i + 1) % count, i) for i in range(ends)])  5.77 us
    ppermute x1, starting transfers between devices, extended(): lax.ppermute(head, axis, [((i + 1) % count, i) for i in range(ends)])  4.82 us
    ppermute x3, starting transfers between devices, shifted(): return lax.ppermute(block, axis, route)  4.8 us
    ppermute x7, starting transfers between devices, _convert_stocks(): column.append(ppermute(column[-1], axis_name=mesh_dim, perm=row_list))  3.78 us
    slice x6, local copies, waits for them, and re-layouts, body(): keys_all[j:j + frames]  3.52 us
  transfers between devices with their start and end apart: 14, of which 9 were waited for; matrix products, arithmetic and copies ran while one was open for 25% of the time, Pallas kernels for 0%

profile of v1, /device:TPU:18, one launch (start us, length us, event | category | flops | bytes accessed | tf_op | source)
XLA Modules:
  0.0 146.6 jit_solution(3433694857812090252)
XLA Ops:
  6.5 0.7 all-gather.3.cloned.1.call-update
  7.3 1.6 %collective-permute-start = (bf16[512,192]{0,1:T(8,128)(2,1)}, bf16[512,192]{0,1:T(8,128)(2,1)S(1)}, u32[]{:S(2)}, u32[]{:S(2)}) collective-permute-start(bf16[512,192]{0,1:T(8,128)(2,1)} %param.19), channel_id=1, source_target_pairs={{0,1},{1,2},{2,3},{3,4},{4,5},{5,6},{6,7},{7,0},{8,9},{9,10},{10,1... | collective-permute-start | bytes 589832 | tf_op jit(solution)/shard_map/ppermute | solution.py:34
  8.9 0.9 bitcast_dynamic-update-slice_fusion.7
  10.6 1.0 fusion.24
  11.6 0.8 multiply_bitcast_fusion.1
  12.4 1.4 fusion.55
  13.8 0.7 iota_compare_fusion.4
  14.5 1.3 iota_compare_fusion.2
  16.2 1.6 %collective-permute-start.1 = (bf16[512,192]{0,1:T(8,128)(2,1)S(1)}, bf16[512,192]{0,1:T(8,128)(2,1)S(1)}, u32[]{:S(2)}, u32[]{:S(2)}) collective-permute-start(bf16[512,192]{0,1:T(8,128)(2,1)S(1)} %collective-permute-done), channel_id=1, source_target_pairs={{0,1},{1,2},{2,3},{3,4},{4,5},{5,6},{6,7},{7,0},{8,9},{9,10},{10,1... | collective-permute-start | bytes 589832 | tf_op jit(solution)/shard_map/ppermute | solution.py:34
  17.8 8.0 %collective-permute-done.1 = bf16[512,192]{0,1:T(8,128)(2,1)S(1)} collective-permute-done((bf16[512,192]{0,1:T(8,128)(2,1)S(1)}, bf16[512,192]{0,1:T(8,128)(2,1)S(1)}, u32[]{:S(2)}, u32[]{:S(2)}) %collective-permute-start.1) | collective-permute-done | bytes 196640 | tf_op jit(solution)/shard_map/ppermute | solution.py:34
  25.8 0.6 collective-permute-start.2
  26.4 8.4 %collective-permute-done.2 = bf16[512,192]{0,1:T(8,128)(2,1)S(1)} collective-permute-done((bf16[512,192]{0,1:T(8,128)(2,1)S(1)}, bf16[512,192]{0,1:T(8,128)(2,1)S(1)}, u32[]{:S(2)}, u32[]{:S(2)}) %collective-permute-start.2) | collective-permute-done | bytes 196640 | tf_op jit(solution)/shard_map/ppermute | solution.py:34
  34.8 6.5 %collective-permute-done.3 = bf16[512,192]{0,1:T(8,128)(2,1)S(1)} collective-permute-done((bf16[512,192]{0,1:T(8,128)(2,1)S(1)}, bf16[512,192]{0,1:T(8,128)(2,1)S(1)}, u32[]{:S(2)}, u32[]{:S(2)}) %collective-permute-start.3) | collective-permute-done | bytes 196640 | tf_op jit(solution)/shard_map/ppermute | solution.py:34
  41.4 12.6 %collective-permute-done.4 = bf16[512,192]{0,1:T(8,128)(2,1)S(1)} collective-permute-done((bf16[512,192]{0,1:T(8,128)(2,1)S(1)}, bf16[512,192]{0,1:T(8,128)(2,1)S(1)}, u32[]{:S(2)}, u32[]{:S(2)}) %collective-permute-start.4) | collective-permute-done | bytes 196640 | tf_op jit(solution)/shard_map/ppermute | solution.py:34
  54.0 9.2 %collective-permute-done.5 = bf16[512,192]{0,1:T(8,128)(2,1)S(1)} collective-permute-done((bf16[512,192]{0,1:T(8,128)(2,1)S(1)}, bf16[512,192]{0,1:T(8,128)(2,1)S(1)}, u32[]{:S(2)}, u32[]{:S(2)}) %collective-permute-start.5) | collective-permute-done | bytes 196640 | tf_op jit(solution)/shard_map/ppermute | solution.py:34
  63.2 7.2 %collective-permute-done.6 = bf16[512,192]{0,1:T(8,128)(2,1)S(1)} collective-permute-done((bf16[512,192]{0,1:T(8,128)(2,1)S(1)}, bf16[512,192]{0,1:T(8,128)(2,1)S(1)}, u32[]{:S(2)}, u32[]{:S(2)}) %collective-permute-start.6) | collective-permute-done | bytes 196640 | tf_op jit(solution)/shard_map/ppermute | solution.py:34
  70.5 0.6 gather_fusion
  71.1 0.3 copy-done
  71.4 0.7 convolution_bitcast_fusion.1
  72.2 0.2 copy.43
  73.4 1.9 %collective-permute-start.7 = (bf16[2,1,1,180,512]{4,3,2,1,0:T(8,128)(2,1)S(1)}, bf16[2,1,1,180,512]{4,3,2,1,0:T(8,128)(2,1)S(1)}, u32[]{:S(2)}, u32[]{:S(2)}) collective-permute-start(bf16[2,1,1,180,512]{4,3,2,1,0:T(8,128)(2,1)S(1)} %pad_maximum_fusion.1), channel_id=1, source_target_pairs={{0,1},{1,2},{2,3},{3,4},{4,5},{5,6},{6,7},{8,9},{9,10},{10,11},{11... | collective-permute-start | bytes 1105928 | tf_op jit(solution)/shard_map/ppermute | solution.py:52
  75.3 4.8 %collective-permute-start.8 = (bf16[2,1,1,180,512]{4,3,2,1,0:T(8,128)(2,1)S(1)}, bf16[2,1,1,180,512]{4,3,2,1,0:T(8,128)(2,1)S(1)}, u32[]{:S(2)}, u32[]{:S(2)}) collective-permute-start(bf16[2,1,1,180,512]{4,3,2,1,0:T(8,128)(2,1)S(1)} %pad_maximum_fusion.1), channel_id=1, source_target_pairs={{1,0},{2,1},{3,2},{4,3},{5,4},{6,5},{7,6},{9,8},{10,9},{11,10},{12... | collective-permute-start | bytes 1105928 | tf_op jit(solution)/shard_map/ppermute | solution.py:54
  81.1 0.4 fusion.34
  81.4 0.2 reshape.432
  81.7 9.7 %collective-permute-done.7 = bf16[2,1,1,180,512]{4,3,2,1,0:T(8,128)(2,1)S(1)} collective-permute-done((bf16[2,1,1,180,512]{4,3,2,1,0:T(8,128)(2,1)S(1)}, bf16[2,1,1,180,512]{4,3,2,1,0:T(8,128)(2,1)S(1)}, u32[]{:S(2)}, u32[]{:S(2)}) %collective-permute-start.7) | collective-permute-done | bytes 368672 | tf_op jit(solution)/shard_map/ppermute | solution.py:52
  91.4 5.8 %collective-permute-done.8 = bf16[2,1,1,180,512]{4,3,2,1,0:T(8,128)(2,1)S(1)} collective-permute-done((bf16[2,1,1,180,512]{4,3,2,1,0:T(8,128)(2,1)S(1)}, bf16[2,1,1,180,512]{4,3,2,1,0:T(8,128)(2,1)S(1)}, u32[]{:S(2)}, u32[]{:S(2)}) %collective-permute-start.8) | collective-permute-done | bytes 368672 | tf_op jit(solution)/shard_map/ppermute | solution.py:54
  97.4 1.2 fusion.16
  98.6 0.2 slice.150
  98.8 0.3 copy.50
  99.1 0.2 slice.152
  99.3 0.3 copy.51
  99.7 0.2 slice.154
  99.9 0.3 copy.52
  100.3 0.2 slice.136
  100.5 1.1 copy.45
  101.5 0.2 slice.138
  101.8 1.1 copy.46
  102.8 0.2 slice.140
  103.1 1.0 copy.47
  104.1 0.8 convolution_multiply_fusion
  104.9 0.8 fusion.69
  105.7 2.1 %convolution_bitcast_fusion = f32[1,1,180,1536]{3,2,1,0:T(8,128)S(1)} fusion(bf16[512,1536]{0,1:T(8,128)(2,1)} %all-gather.3.cloned.1.call-done, bf16[1,1,180,512]{3,2,1,0:T(8,128)(2,1)S(1)} %copy-done, f32[512]{0:T(512)S(1)} %copy-done.5, f32[180]{0:T(256)S(1)} %add_rsqrt_fusion.4), kind=kOutput, calls=%fused_computation.2 | convolution fusion | flops 283484160 | bytes 2865872 | tf_op jit(solution)/shard_map/dot_general | solution.py:197
  107.8 0.9 slice_multiply_fusion
  108.7 0.7 slice_bitcast_fusion.2
  109.4 1.2 copy.55
  110.7 0.9 copy.56
  111.6 1.2 copy.61
  113.0 0.9 copy.62
  113.9 1.3 multiply_convert_fusion
  115.2 0.8 pad_maximum_fusion.2
  116.0 1.4 collective-permute-start.9
  117.5 1.5 collective-permute-start.10
  118.9 1.5 %convolution_bitcast_fusion.2 = bf16[1,3,60,8,64]{2,4,3,1,0:T(8,128)(2,1)} fusion(bf16[1,3,60,8,64]{2,4,3,1,0:T(8,128)(2,1)S(1)} %copy-done.4, bf16[1,3,60,8,64]{2,4,3,1,0:T(8,128)(2,1)S(1)} %copy-done.3, bf16[1,3,60,8,64]{2,4,3,1,0:T(8,128)(2,1)S(1)} %copy-done.2, f32[3,8,60,180]{3,2,1,0:T(8,128)S(1)} %get-tuple-element.37, ...), kind=kOutput, calls=%fused_computation.11 | convolution fusion | flops 35354880 | bytes 1779840 | tf_op jit(solution)/shard_map/rwhqk,rwkhd->rwqhd/dot_general | solution.py:134
  120.5 1.3 copy.54
  121.8 0.2 reshape.434
  122.0 0.4 fusion.38
  122.4 1.9 %collective-permute-start.11 = (bf16[2,1,1,180,512]{4,3,2,1,0:T(8,128)(2,1)}, bf16[2,1,1,180,512]{4,3,2,1,0:T(8,128)(2,1)}, u32[]{:S(2)}, u32[]{:S(2)}) collective-permute-start(bf16[2,1,1,180,512]{4,3,2,1,0:T(8,128)(2,1)} %pad_maximum_fusion.2), channel_id=1, source_target_pairs={{0,8},{8,16},{16,24},{1,9},{9,17},{17,25},{2,10},{10,18},{18,26},{... | collective-permute-start | bytes 1105928 | tf_op jit(solution)/shard_map/ppermute | solution.py:64
  124.8 1.0 fusion.66
  126.0 7.3 %collective-permute-done.10 = bf16[2,1,1,180,512]{4,3,2,1,0:T(8,128)(2,1)} collective-permute-done((bf16[2,1,1,180,512]{4,3,2,1,0:T(8,128)(2,1)}, bf16[2,1,1,180,512]{4,3,2,1,0:T(8,128)(2,1)}, u32[]{:S(2)}, u32[]{:S(2)}) %collective-permute-start.10) | collective-permute-done | bytes 368672 | tf_op jit(solution)/shard_map/ppermute | solution.py:64
  133.4 1.0 fusion.67
  134.6 1.0 fusion.68
  136.2 0.3 multiply_reduce_fusion.1
  136.8 0.3 multiply_reduce_fusion
  137.2 2.5 %fusion.20 = bf16[1,1,180,512]{3,2,1,0:T(8,128)(2,1)} fusion(bf16[1,1,180,512]{3,2,1,0:T(8,128)(2,1)S(1)} %copy-done.6, bf16[1,1,180,512]{3,2,1,0:T(8,128)(2,1)S(1)} %copy-done, bf16[1024,512]{0,1:T(8,128)(2,1)} %all-gather.5.cloned.1.call-done, bf16[180,512]{1,0:T(8,128)(2,1)S(1)} %copy.68, bf16[180,512]{1,0:T(8,128)(2,1)S(1)} %fusion.38, f32[]{:T(128)} %bitcast.62, ...), kind=kOutput, calls=%fused_computation.48 | convolution fusion | flops 190863360 | bytes 1970193 | tf_op jit(solution)/shard_map/dot_general | solution.py:247
  (84 shorter events, 4.0 us)
Async XLA Ops:
  6.5 99.2 %all-gather.3.cloned.1.call-start = ((), (), s32[]{:S(2)}) async-start(), calls=%async_computation | async-start | bytes 1769472 | tf_op jit(solution)/shard_map/all_gather | solution.py:199
  7.3 130.0 %all-gather.5.cloned.1.call-start = ((), (), s32[]{:S(2)}) async-start(), calls=%async_computation.1 | async-start | bytes 1179648 | tf_op jit(solution)/shard_map/all_gather | solution.py:249
  7.3 8.9 %collective-permute-start = (bf16[512,192]{0,1:T(8,128)(2,1)}, bf16[512,192]{0,1:T(8,128)(2,1)S(1)}, u32[]{:S(2)}, u32[]{:S(2)}) collective-permute-start(bf16[512,192]{0,1:T(8,128)(2,1)} %param.19), channel_id=1, source_target_pairs={{0,1},{1,2},{2,3},{3,4},{4,5},{5,6},{6,7},{7,0},{8,9},{9,10},{10,1... | collective-permute-start | bytes 589832 | tf_op jit(solution)/shard_map/ppermute | solution.py:34
  16.2 9.6 %collective-permute-start.1 = (bf16[512,192]{0,1:T(8,128)(2,1)S(1)}, bf16[512,192]{0,1:T(8,128)(2,1)S(1)}, u32[]{:S(2)}, u32[]{:S(2)}) collective-permute-start(bf16[512,192]{0,1:T(8,128)(2,1)S(1)} %collective-permute-done), channel_id=1, source_target_pairs={{0,1},{1,2},{2,3},{3,4},{4,5},{5,6},{6,7},{7,0},{8,9},{9,10},{10,1... | collective-permute-start | bytes 589832 | tf_op jit(solution)/shard_map/ppermute | solution.py:34
  25.8 9.0 %collective-permute-start.2 = (bf16[512,192]{0,1:T(8,128)(2,1)S(1)}, bf16[512,192]{0,1:T(8,128)(2,1)S(1)}, u32[]{:S(2)}, u32[]{:S(2)}) collective-permute-start(bf16[512,192]{0,1:T(8,128)(2,1)S(1)} %collective-permute-done.1), channel_id=1, source_target_pairs={{0,1},{1,2},{2,3},{3,4},{4,5},{5,6},{6,7},{7,0},{8,9},{9,10},{10,1... | collective-permute-start | bytes 589832 | tf_op jit(solution)/shard_map/ppermute | solution.py:34
  34.8 6.6 %collective-permute-start.3 = (bf16[512,192]{0,1:T(8,128)(2,1)S(1)}, bf16[512,192]{0,1:T(8,128)(2,1)S(1)}, u32[]{:S(2)}, u32[]{:S(2)}) collective-permute-start(bf16[512,192]{0,1:T(8,128)(2,1)S(1)} %collective-permute-done.2), channel_id=1, source_target_pairs={{0,1},{1,2},{2,3},{3,4},{4,5},{5,6},{6,7},{7,0},{8,9},{9,10},{10,1... | collective-permute-start | bytes 589832 | tf_op jit(solution)/shard_map/ppermute | solution.py:34
  41.4 12.6 %collective-permute-start.4 = (bf16[512,192]{0,1:T(8,128)(2,1)S(1)}, bf16[512,192]{0,1:T(8,128)(2,1)S(1)}, u32[]{:S(2)}, u32[]{:S(2)}) collective-permute-start(bf16[512,192]{0,1:T(8,128)(2,1)S(1)} %collective-permute-done.3), channel_id=1, source_target_pairs={{0,1},{1,2},{2,3},{3,4},{4,5},{5,6},{6,7},{7,0},{8,9},{9,10},{10,1... | collective-permute-start | bytes 589832 | tf_op jit(solution)/shard_map/ppermute | solution.py:34
  54.0 9.2 %collective-permute-start.5 = (bf16[512,192]{0,1:T(8,128)(2,1)S(1)}, bf16[512,192]{0,1:T(8,128)(2,1)S(1)}, u32[]{:S(2)}, u32[]{:S(2)}) collective-permute-start(bf16[512,192]{0,1:T(8,128)(2,1)S(1)} %collective-permute-done.4), channel_id=1, source_target_pairs={{0,1},{1,2},{2,3},{3,4},{4,5},{5,6},{6,7},{7,0},{8,9},{9,10},{10,1... | collective-permute-start | bytes 589832 | tf_op jit(solution)/shard_map/ppermute | solution.py:34
  63.2 7.2 %collective-permute-start.6 = (bf16[512,192]{0,1:T(8,128)(2,1)S(1)}, bf16[512,192]{0,1:T(8,128)(2,1)S(1)}, u32[]{:S(2)}, u32[]{:S(2)}) collective-permute-start(bf16[512,192]{0,1:T(8,128)(2,1)S(1)} %collective-permute-done.5), channel_id=1, source_target_pairs={{0,1},{1,2},{2,3},{3,4},{4,5},{5,6},{6,7},{7,0},{8,9},{9,10},{10,1... | collective-permute-start | bytes 589832 | tf_op jit(solution)/shard_map/ppermute | solution.py:34
  70.5 0.9 copy-start
  70.5 0.9 copy-start.5
  73.4 17.9 %collective-permute-start.7 = (bf16[2,1,1,180,512]{4,3,2,1,0:T(8,128)(2,1)S(1)}, bf16[2,1,1,180,512]{4,3,2,1,0:T(8,128)(2,1)S(1)}, u32[]{:S(2)}, u32[]{:S(2)}) collective-permute-start(bf16[2,1,1,180,512]{4,3,2,1,0:T(8,128)(2,1)S(1)} %pad_maximum_fusion.1), channel_id=1, source_target_pairs={{0,1},{1,2},{2,3},{3,4},{4,5},{5,6},{6,7},{8,9},{9,10},{10,11},{11... | collective-permute-start | bytes 1105928 | tf_op jit(solution)/shard_map/ppermute | solution.py:52
  75.3 21.8 %collective-permute-start.8 = (bf16[2,1,1,180,512]{4,3,2,1,0:T(8,128)(2,1)S(1)}, bf16[2,1,1,180,512]{4,3,2,1,0:T(8,128)(2,1)S(1)}, u32[]{:S(2)}, u32[]{:S(2)}) collective-permute-start(bf16[2,1,1,180,512]{4,3,2,1,0:T(8,128)(2,1)S(1)} %pad_maximum_fusion.1), channel_id=1, source_target_pairs={{1,0},{2,1},{3,2},{4,3},{5,4},{6,5},{7,6},{9,8},{10,9},{11,10},{12... | collective-permute-start | bytes 1105928 | tf_op jit(solution)/shard_map/ppermute | solution.py:54
  113.9 1.4 copy-start.1
  113.9 5.0 %copy-start.2 = (bf16[1,3,60,8,64]{2,4,3,1,0:T(8,128)(2,1)S(1)}, bf16[1,3,60,8,64]{2,4,3,1,0:T(8,128)(2,1)}, u32[]{:S(2)}) copy-start(bf16[1,3,60,8,64]{2,4,3,1,0:T(8,128)(2,1)} %copy.45) | copy-start | bytes 552964
  113.9 5.1 %copy-start.3 = (bf16[1,3,60,8,64]{2,4,3,1,0:T(8,128)(2,1)S(1)}, bf16[1,3,60,8,64]{2,4,3,1,0:T(8,128)(2,1)}, u32[]{:S(2)}) copy-start(bf16[1,3,60,8,64]{2,4,3,1,0:T(8,128)(2,1)} %copy.46) | copy-start | bytes 552964
  113.9 5.1 %copy-start.4 = (bf16[1,3,60,8,64]{2,4,3,1,0:T(8,128)(2,1)S(1)}, bf16[1,3,60,8,64]{2,4,3,1,0:T(8,128)(2,1)}, u32[]{:S(2)}) copy-start(bf16[1,3,60,8,64]{2,4,3,1,0:T(8,128)(2,1)} %copy.47) | copy-start | bytes 552964
  116.0 8.8 %collective-permute-start.9 = (bf16[2,1,1,180,512]{4,3,2,1,0:T(8,128)(2,1)}, bf16[2,1,1,180,512]{4,3,2,1,0:T(8,128)(2,1)}, u32[]{:S(2)}, u32[]{:S(2)}) collective-permute-start(bf16[2,1,1,180,512]{4,3,2,1,0:T(8,128)(2,1)} %pad_maximum_fusion.2), channel_id=1, source_target_pairs={{0,24},{1,25},{2,26},{3,27},{4,28},{5,29},{6,30},{7,31}} | collective-permute-start | bytes 1105928 | tf_op jit(solution)/shard_map/ppermute | solution.py:64
  117.5 15.9 %collective-permute-start.10 = (bf16[2,1,1,180,512]{4,3,2,1,0:T(8,128)(2,1)}, bf16[2,1,1,180,512]{4,3,2,1,0:T(8,128)(2,1)}, u32[]{:S(2)}, u32[]{:S(2)}) collective-permute-start(bf16[2,1,1,180,512]{4,3,2,1,0:T(8,128)(2,1)} %pad_maximum_fusion.2), channel_id=1, source_target_pairs={{0,16},{8,24},{1,17},{9,25},{2,18},{10,26},{3,19},{11,27},{4,20},{... | collective-permute-start | bytes 1105928 | tf_op jit(solution)/shard_map/ppermute | solution.py:64
  122.4 12.2 %collective-permute-start.11 = (bf16[2,1,1,180,512]{4,3,2,1,0:T(8,128)(2,1)}, bf16[2,1,1,180,512]{4,3,2,1,0:T(8,128)(2,1)}, u32[]{:S(2)}, u32[]{:S(2)}) collective-permute-start(bf16[2,1,1,180,512]{4,3,2,1,0:T(8,128)(2,1)} %pad_maximum_fusion.2), channel_id=1, source_target_pairs={{0,8},{8,16},{16,24},{1,9},{9,17},{17,25},{2,10},{10,18},{18,26},{... | collective-permute-start | bytes 1105928 | tf_op jit(solution)/shard_map/ppermute | solution.py:64
  136.2 1.1 copy-start.6
Sparse Core Ops, SparseCore 0:
  9.5 51.6 all-gather.2
  63.4 41.5 all-gather.4
